TPU v7x, 512 devices: a whole 4x4x16 slice. The times are simulated.
512 devices in a mesh: dp: 32 (over x, y, core), tensor: 16 (over z).
Axes of the slice: x: 4, y: 4, z: 16, core: 2. Of those that a mesh axis runs over, the one named last changes fastest.
Arguments:
- tokens: bfloat16 [2048, 16384], P('dp', 'tensor'), parts along dimension 0, may hold values from -6 to 6
- gate_up_base: bfloat16 [2048, 2, 53248], P('dp', None, 'tensor'), parts along dimension 0, may hold values from -6 to 6
- shrink_gate_up: bfloat16 [64, 2, 16384, 64], P('dp', None, 'tensor'), parts along dimension 0, may hold values from -0.046875 to 0.046875
- expand_gate_up: bfloat16 [64, 2, 64, 53248], P('dp', None, None, 'tensor'), parts along dimension 0, may hold values from -0.75 to 0.75
- shrink_down: bfloat16 [64, 53248, 64], P('dp', 'tensor'), parts along dimension 0, may hold values from -0.02734375 to 0.02734375
- expand_down: bfloat16 [64, 64, 16384], P('dp', None, 'tensor'), parts along dimension 0, may hold values from -0.75 to 0.75
- token_slot: int32 [2048], P('dp'), parts along dimension 0, may hold values from 0 to 1, never falling along the last dimension, each value on 1 to 48 neighbouring positions
Outputs:
- hidden: bfloat16 [2048, 53248], P('dp', 'tensor'), parts along dimension 0
- down_delta: bfloat16 [2048, 16384], P('dp', 'tensor'), parts along dimension 0
There are 32 independent parts, one for each index of `dp`. A program takes and returns all parts, laid end to end along the dimension named above; each array names one. Nothing has to cross between parts.
Inputs may be any that keep to these rules, and one draw needn't show every extreme that they name: `token_slot`: slots never fall along the tokens; each of the 2 slots holds 1 to 48 tokens.
All inputs are finite; a program needn't handle non-finite values.
Results may differ from a plain program's by a relative error of at most 0.017.
Values may be sent and summed in bfloat16 or wider, within the bound.
A program may use at most 64 MiB of HBM per device.

v0:
```python
import jax
import jax.numpy as jnp
from jax import lax
from jax.sharding import PartitionSpec as P


def per_device(
    tokens, gate_up_base, shrink_gate_up, expand_gate_up, shrink_down, expand_down, token_slot
):
    slot_count = shrink_gate_up.shape[0]
    selector = (token_slot[:, None] == jnp.arange(slot_count, dtype=jnp.int32)[None, :]).astype(
        jnp.float32
    )
    partial_up = jnp.einsum(
        "td,agdr->tagr", tokens, shrink_gate_up, preferred_element_type=jnp.float32
    )
    partial_up = jnp.sum(partial_up * selector[:, :, None, None], axis=1)
    shrunk = lax.psum(partial_up, "tensor").astype(jnp.bfloat16)
    widened = jnp.einsum(
        "tgr,agrf->tagf", shrunk, expand_gate_up, preferred_element_type=jnp.float32
    )
    preact = gate_up_base.astype(jnp.float32) + jnp.sum(
        widened * selector[:, :, None, None], axis=1
    )
    hidden = (jax.nn.silu(preact[:, 0]) * preact[:, 1]).astype(jnp.bfloat16)
    narrowed = jnp.einsum("tf,afr->tar", hidden, shrink_down, preferred_element_type=jnp.float32)
    partial_down = jnp.sum(narrowed * selector[:, :, None], axis=1)
    reduced = lax.psum(partial_down, "tensor").astype(jnp.bfloat16)
    expanded = jnp.einsum("tr,ard->tad", reduced, expand_down, preferred_element_type=jnp.float32)
    down_delta = jnp.sum(expanded * selector[:, :, None], axis=1).astype(jnp.bfloat16)
    return (hidden, down_delta)


def solution(mesh):
    placed = (
        P("dp", "tensor"),
        P("dp", None, "tensor"),
        P("dp", None, "tensor", None),
        P("dp", None, None, "tensor"),
        P("dp", "tensor", None),
        P("dp", None, "tensor"),
        P("dp"),
    )
    return jax.shard_map(
        per_device,
        mesh=mesh,
        in_specs=placed,
        out_specs=(P("dp", "tensor"), P("dp", "tensor")),
        check_vma=False,
    )
```

profile of v0, /device:TPU:6, one launch (start us, length us, event | category | flops | bytes accessed | tf_op | source)
XLA Modules:
  0.0 121.6 jit_solution(14846713409881743834)
XLA Ops:
  0.6 0.0 copy-start
  0.6 0.8 compare_convert_fusion
  1.4 1.5 %fusion.3 = f32[64,2,64]{2,0,1:T(8,128)S(1)} fusion(bf16[2,2,1024,64]{2,3,1,0:T(8,128)(2,1)} %param.9, bf16[64,1024]{1,0:T(8,128)(2,1)} %param.7, f32[64,2]{0,1:T(2,128)S(1)} %compare_convert_fusion), kind=kOutput, calls=%fused_computation.7 | convolution fusion | flops 33579008 | bytes 688640 | tf_op jit(solution)/shard_map/td,agdr->tagr/dot_general | solution.py:14
  2.9 62.1 %psum.14 = bf16[64,2,64]{2,0,1:T(8,128)(2,1)S(1)} all-reduce(f32[64,2,64]{2,0,1:T(8,128)S(1)} %fusion.3), channel_id=1, replica_groups=mesh['dp'=32,'tensor'=16] {'tensor'}, use_global_device_ids=true, to_apply=%region_1.0 | all-reduce | flops 8192 | bytes 49152 | tf_op jit(solution)/shard_map/psum | solution.py:18
  65.0 0.0 copy-done
  65.0 0.0 copy-start.2
  65.0 0.6 fusion
  65.6 0.6 copy-done.2
  66.2 0.2 bitcast_add_fusion
  66.4 0.0 copy-start.3
  66.4 0.0 copy-start.4
  66.4 0.2 fusion.6
  66.6 0.9 copy-done.3
  67.5 0.0 copy-start.1
  67.5 0.5 fusion.4
  68.1 52.7 %psum.15 = bf16[64,64]{1,0:T(8,128)(2,1)S(1)} all-reduce(f32[64,64]{1,0:T(8,128)S(1)} %fusion.4), channel_id=1, replica_groups=mesh['dp'=32,'tensor'=16] {'tensor'}, use_global_device_ids=true, to_apply=%region_4.5 | all-reduce | flops 4096 | bytes 24576 | tf_op jit(solution)/shard_map/psum | solution.py:28
  120.7 0.0 copy-done.4
  120.7 0.9 fusion.2
  121.6 0.0 copy-done.1
Async XLA Ops:
  0.6 64.4 %copy-start = (bf16[2,2,64,3328]{3,2,1,0:T(8,128)(2,1)S(1)}, bf16[2,2,64,3328]{3,2,1,0:T(8,128)(2,1)}, u32[]{:S(2)}) copy-start(bf16[2,2,64,3328]{3,2,1,0:T(8,128)(2,1)} %param.10) | copy-start | bytes 5111812
  65.0 1.2 copy-start.2
  66.4 1.2 copy-start.3
  66.4 54.4 %copy-start.4 = (bf16[2,64,1024]{2,1,0:T(8,128)(2,1)S(1)}, bf16[2,64,1024]{2,1,0:T(8,128)(2,1)}, u32[]{:S(2)}) copy-start(bf16[2,64,1024]{2,1,0:T(8,128)(2,1)} %param.12) | copy-start | bytes 786436
  67.5 54.1 %copy-start.1 = (bf16[64,3328]{1,0:T(8,128)(2,1)}, bf16[64,3328]{1,0:T(8,128)(2,1)S(1)}, u32[]{:S(2)}) copy-start(bf16[64,3328]{1,0:T(8,128)(2,1)S(1)} %fusion.6) | copy-start | bytes 1277956
where the time goes:
time: 122 us
  blocking collectives  115 us (94%)
  matrix products  3.49 us (3%)
  local copies, waits for them, and re-layouts  1.48 us (1%)
    psum x1, blocking collectives, per_device(): shrunk = lax.psum(partial_up, 'tensor').astype(jnp.bfloat16)  62.1 us
    psum x1, blocking collectives, per_device(): reduced = lax.psum(partial_down, 'tensor').astype(jnp.bfloat16)  52.7 us

commit v1 on v0

v1 whole, which is shorter than its diff:
```python
import functools

import jax
import jax.numpy as jnp
from jax import lax
from jax.experimental import pallas as pl
from jax.experimental.pallas import tpu as pltpu
from jax.sharding import PartitionSpec as P

MESH = pl.DeviceIdType.MESH
NT = (((1,), (1,)), ((), ()))


def nt_dot(a, b):
    return lax.dot_general(a, b, NT, preferred_element_type=jnp.float32)


def dot(a, b):
    return jnp.dot(a, b, preferred_element_type=jnp.float32)


def kernel(
    tokens_hbm, base_hbm, shrink_up_hbm, expand_up_hbm, shrink_down_hbm, expand_down_hbm, slot_hbm,
    hidden_out, down_out,
    tokens, base, shrink_up, expand_up, shrink_down, expand_down, slot,
    planar, hidden, down,
    part, land_a, mine, land_b, part_down, land_c,
    in_sem, out_sem, send_a, recv_a, send_b, recv_b, send_c, recv_c,
):
    me = lax.axis_index("tensor")
    dp = lax.axis_index("dp")
    n = 16
    cube, spot = me // 4, me % 4

    def load(i, src, dst):
        c = pltpu.make_async_copy(src, dst, in_sem.at[i])
        c.start()
        return c

    def peer(z):
        return dict(device_id=(dp, z), device_id_type=MESH)

    def arrived(landing, sem):
        fifteen = landing.at[pl.ds(0, n - 1)]
        pltpu.make_async_copy(fifteen, fifteen, sem).wait()

    barrier = pltpu.get_barrier_semaphore()
    far_first = [8, 7, 9, 6, 10, 5, 11, 4, 12, 3, 13, 2, 14, 1, 15]
    for off in far_first:
        pl.semaphore_signal(barrier, inc=1, **peer((me + off) % n))

    first = [load(0, tokens_hbm, tokens), load(1, shrink_up_hbm, shrink_up), load(2, slot_hbm, slot)]
    second = [load(3, base_hbm, base), load(4, expand_up_hbm, expand_up)]
    third = [load(5, shrink_down_hbm, shrink_down), load(6, expand_down_hbm, expand_down)]
    for c in first:
        c.wait()

    ones = jnp.sum(slot[...].astype(jnp.float32), axis=1, keepdims=True)
    row = lax.broadcasted_iota(jnp.int32, (64, 128), 0).astype(jnp.float32)
    second_slot = row >= 64.0 - ones
    lane_low = lax.broadcasted_iota(jnp.int32, (64, 128), 1) < 64
    keep = lane_low != second_slot

    both = nt_dot(tokens[...], shrink_up[...])
    part[...] = jnp.where(second_slot, both[:, 128:], both[:, :128])

    pl.semaphore_wait(barrier, n - 1)

    copies = []
    for off in (1, 2, 3):
        to = (spot + off) % 4
        c = pltpu.make_async_remote_copy(
            src_ref=part.at[pl.ds(pl.multiple_of(to * 16, 16), 16)],
            dst_ref=land_a.at[off - 1],
            send_sem=send_a.at[off - 1],
            recv_sem=recv_a.at[off - 1],
            **peer(cube * 4 + to),
        )
        c.start()
        copies.append(c)

    for c in second:
        c.wait()
    planar[0] = base[:, 0, :].astype(jnp.float32)
    planar[1] = base[:, 1, :].astype(jnp.float32)

    own = pl.ds(pl.multiple_of(spot * 16, 16), 16)
    total = part[own, :]
    for c in copies:
        c.wait_recv()
    for i in range(3):
        total += land_a[i]
    mine[...] = total.astype(jnp.bfloat16)

    copies_b = []
    for i, off in enumerate(far_first):
        c = pltpu.make_async_remote_copy(
            src_ref=mine,
            dst_ref=land_b.at[me],
            send_sem=send_b.at[i],
            recv_sem=recv_b,
            **peer((me + off) % n),
        )
        c.start()
        copies_b.append(c)
    land_b[me] = mine[...]
    for c in third:
        c.wait()
    arrived(land_b, recv_b)

    shrunk = land_b[pl.ds(0, 4)].astype(jnp.float32)
    for i in range(1, 4):
        shrunk += land_b[pl.ds(4 * i, 4)].astype(jnp.float32)
    shrunk = shrunk.reshape(64, 128)
    swapped = pltpu.roll(shrunk, 64, 1)
    lhs = [
        jnp.where(keep, jnp.where(lane_low, shrunk, swapped), 0.0).astype(jnp.bfloat16),
        jnp.where(keep, jnp.where(lane_low, swapped, shrunk), 0.0).astype(jnp.bfloat16),
    ]
    narrowed = jnp.zeros((64, 128), jnp.float32)
    for k in range(13):
        cols = pl.ds(k * 256, 256)
        gate = dot(lhs[0], jnp.concatenate([expand_up[0, 0, :, cols], expand_up[1, 0, :, cols]], axis=0))
        up = dot(lhs[1], jnp.concatenate([expand_up[0, 1, :, cols], expand_up[1, 1, :, cols]], axis=0))
        gate += planar[0, :, cols]
        up += planar[1, :, cols]
        h = (gate / (1.0 + jnp.exp(-gate)) * up).astype(jnp.bfloat16)
        hidden[:, cols] = h
        narrowed += nt_dot(h, shrink_down[:, cols])
    write_hidden = pltpu.make_async_copy(hidden, hidden_out, out_sem.at[0])
    write_hidden.start()

    turned = pltpu.roll(narrowed, 64, 1)
    low = jnp.where(second_slot, turned, narrowed)[:32]
    high = jnp.where(second_slot, narrowed, turned)[32:]
    part_down[...] = jnp.where(lane_low[:32], low, high).astype(jnp.bfloat16)
    copies_c = []
    for i, off in enumerate(far_first):
        c = pltpu.make_async_remote_copy(
            src_ref=part_down,
            dst_ref=land_c.at[me],
            send_sem=send_c.at[i],
            recv_sem=recv_c,
            **peer((me + off) % n),
        )
        c.start()
        copies_c.append(c)
    land_c[me] = part_down[...]
    arrived(land_c, recv_c)
    packed = land_c[0].astype(jnp.float32)
    for i in range(1, n):
        packed += land_c[i].astype(jnp.float32)
    other = pltpu.roll(packed, 64, 1)
    reduced = jnp.concatenate(
        [jnp.where(lane_low[:32], packed, other), jnp.where(lane_low[:32], other, packed)], axis=0
    )
    reduced = jnp.where(keep, reduced, 0.0).astype(jnp.bfloat16)
    down[...] = dot(reduced, expand_down[...]).astype(jnp.bfloat16)
    write_down = pltpu.make_async_copy(down, down_out, out_sem.at[1])
    write_down.start()
    for c in copies + copies_b + copies_c:
        c.wait_send()
    write_hidden.wait()
    write_down.wait()


def per_device(
    tokens, gate_up_base, shrink_gate_up, expand_gate_up, shrink_down, expand_down, token_slot
):
    shrink_up = jnp.swapaxes(shrink_gate_up, 2, 3).reshape(256, 1024)
    down_t = jnp.swapaxes(shrink_down, 1, 2).reshape(128, 3328)
    expand_d = expand_down.reshape(128, 1024)
    slot = token_slot.reshape(1, 64)
    bf, f32 = jnp.bfloat16, jnp.float32
    dma = pltpu.SemaphoreType.DMA
    return pl.pallas_call(
        kernel,
        out_shape=(
            jax.ShapeDtypeStruct((64, 3328), bf),
            jax.ShapeDtypeStruct((64, 1024), bf),
        ),
        in_specs=[pl.BlockSpec(memory_space=pl.ANY)] * 7,
        out_specs=[pl.BlockSpec(memory_space=pl.ANY)] * 2,
        scratch_shapes=[
            pltpu.VMEM((64, 1024), bf),
            pltpu.VMEM((64, 2, 3328), bf),
            pltpu.VMEM((256, 1024), bf),
            pltpu.VMEM((2, 2, 64, 3328), bf),
            pltpu.VMEM((128, 3328), bf),
            pltpu.VMEM((128, 1024), bf),
            pltpu.VMEM((1, 64), jnp.int32),
            pltpu.VMEM((2, 64, 3328), f32),
            pltpu.VMEM((64, 3328), bf),
            pltpu.VMEM((64, 1024), bf),
            pltpu.VMEM((64, 128), f32),
            pltpu.VMEM((3, 16, 128), f32),
            pltpu.VMEM((16, 128), bf),
            pltpu.VMEM((16, 16, 128), bf),
            pltpu.VMEM((32, 128), bf),
            pltpu.VMEM((16, 32, 128), bf),
            dma((7,)),
            dma((2,)),
            dma((3,)),
            dma((3,)),
            dma((15,)),
            dma,
            dma((15,)),
            dma,
        ],
        compiler_params=pltpu.CompilerParams(
            collective_id=0, has_side_effects=True, vmem_limit_bytes=60 * 2**20
        ),
    )(tokens, gate_up_base, shrink_up, expand_gate_up, down_t, expand_d, slot)


def solution(mesh):
    placed = (
        P("dp", "tensor"),
        P("dp", None, "tensor"),
        P("dp", None, "tensor", None),
        P("dp", None, None, "tensor"),
        P("dp", "tensor", None),
        P("dp", None, "tensor"),
        P("dp"),
    )
    return jax.shard_map(
        per_device,
        mesh=mesh,
        in_specs=placed,
        out_specs=(P("dp", "tensor"), P("dp", "tensor")),
        check_vma=False,
    )
```

time: 122 us -> 39.5 us (0.32)
  blocking collectives: 115 us -> 0 us
  Pallas kernels: 0 us -> 35.3 us
  matrix products: 3.49 us -> 0 us
  local copies, waits for them, and re-layouts: 1.48 us -> 3.36 us
    psum x2 -> x0, blocking collectives: 115 us -> none  [the longest x1 62.1 us: per_device(): shrunk = lax.psum(partial_up, 'tensor').astype(jnp.bfloat16)]
    pallas_call x0 -> x1, Pallas kernels: none -> 35.3 us  [per_device(): pl.pallas_call(kernel, out_shape=(jax.ShapeDtypeStruct((64, 3328), bf), j...]
    dot_general x4 -> x0, matrix products: 3.49 us -> none  [the longest x1 1.49 us: per_device(): jnp.einsum('td,agdr->tagr', tokens, shrink_gate_up, preferred_element_typ...]
    unnamed x10 -> x2, local copies, waits for them, and re-layouts: 1.48 us -> 3.36 us
where the time goes in v1:
time: 39.5 us; the launch traced here: 39.3 us
  Pallas kernels  35.3 us (89%)
  local copies, waits for them, and re-layouts  3.36 us (9%)
  between operations  0.64 us (2%)
    pallas_call x1, Pallas kernels, per_device(): pl.pallas_call(kernel, out_shape=(jax.ShapeDtypeStruct((64, 3328), bf), j...  35.3 us
    unnamed x2, local copies, waits for them, and re-layouts  3.36 us

profile of v1, /device:TPU:6, one launch (start us, length us, event | category | flops | bytes accessed | tf_op | source)
XLA Modules:
  0.0 39.3 jit_solution(11990863028043460484)
XLA Ops:
  0.6 35.3 %shard_map.86 = (bf16[64,3328]{1,0:T(8,128)(2,1)}, bf16[64,1024]{1,0:T(8,128)(2,1)}) custom-call(bf16[64,1024]{1,0:T(8,128)(2,1)} %tokens_hbm.1, bf16[64,2,3328]{2,1,0:T(2,128)(2,1)} %base_hbm.1, bf16[256,1024]{1,0:T(8,128)(2,1)} %bitcast.9, bf16[2,2,64,3328]{3,2,1,0:T(8,128)(2,1)} %expand_up_hbm.1, bf16[128,3328]{1,0:T(8,128)(2,1)} %bitcast.8, ...), custom_call_target="tpu_custom_call" | custom-call | tf_op jit(solution)/shard_map/pallas_call | solution.py:176
  35.9 1.8 %copy.11 = bf16[64,3328]{1,0:T(8,128)(2,1)} copy(bf16[64,3328]{1,0:T(8,128)(2,1)} %get-tuple-element.4) | data formatting | bytes 851968
  37.7 1.6 %copy.12 = bf16[64,1024]{1,0:T(8,128)(2,1)} copy(bf16[64,1024]{1,0:T(8,128)(2,1)} %get-tuple-element.5) | data formatting | bytes 262144

commit v2 on v1

v2 whole, which is shorter than its diff:
```python
import functools

import jax
import jax.numpy as jnp
from jax import lax
from jax.experimental import pallas as pl
from jax.experimental.pallas import tpu as pltpu
from jax.sharding import PartitionSpec as P

MESH = pl.DeviceIdType.MESH
NT = (((1,), (1,)), ((), ()))


def nt_dot(a, b):
    return lax.dot_general(a, b, NT, preferred_element_type=jnp.float32)


def dot(a, b):
    return jnp.dot(a, b, preferred_element_type=jnp.float32)


GATES = {
    3: ((1, 0),),
    4: ((0, 2),),
    7: ((2, 0), (3, 1)),
    8: ((1, 1), (0, 1)),
    11: ((3, 0),),
    12: ((2, 1), (1, 2)),
    15: ((0, 0),),
}
RELAY = 7


def kernel(
    tokens_hbm, base_hbm, shrink_up_hbm, expand_up_hbm, shrink_down_hbm, slot_hbm,
    hidden, reduced,
    tokens, base, shrink_up, expand_up, shrink_down, slot,
    planar,
    part, land_m, gate_sum, land_s, part_down, land_c,
    in_sem, send_m, recv_m, send_s, recv_s, send_c, recv_c,
):
    me = lax.axis_index("tensor")
    dp = lax.axis_index("dp")
    n = 16
    cube, spot = me // 4, me % 4

    def load(i, src, dst):
        c = pltpu.make_async_copy(src, dst, in_sem.at[i])
        c.start()
        return c

    def peer(z):
        return dict(device_id=(dp, z), device_id_type=MESH)

    def greet(z):
        pl.semaphore_signal(barrier, inc=1, **peer(z))

    barrier = pltpu.get_barrier_semaphore()
    for dst in range(4):
        @pl.when(cube == dst)
        def _():
            for gate, targets in GATES.items():
                if dst in [c for c, _ in targets]:
                    greet(gate)
    for off in (1, 2, 3):
        greet(cube * 4 + (spot + off) % 4)

    first = [load(0, tokens_hbm, tokens), load(1, shrink_up_hbm, shrink_up), load(2, slot_hbm, slot)]
    second = [load(3, base_hbm, base), load(4, expand_up_hbm, expand_up)]
    third = [load(5, shrink_down_hbm, shrink_down)]

    @pl.when(cube >= 2)
    def _():
        land_s[2] = jnp.zeros((64, 128), jnp.bfloat16)

    for c in first:
        c.wait()

    ones = jnp.sum(slot[...].astype(jnp.float32), axis=1, keepdims=True)
    row = lax.broadcasted_iota(jnp.int32, (64, 128), 0).astype(jnp.float32)
    second_slot = row >= 64.0 - ones
    lane_low = lax.broadcasted_iota(jnp.int32, (64, 128), 1) < 64
    keep = lane_low != second_slot

    both = nt_dot(tokens[...], shrink_up[...])
    cube_sum = jnp.where(second_slot, both[:, 128:], both[:, :128])
    part[...] = cube_sum.astype(jnp.bfloat16)

    greetings = 3
    for gate, targets in GATES.items():
        greetings += jnp.where(me == gate, 4 * len(targets), 0)
    pl.semaphore_wait(barrier, greetings)

    mates = []
    for off in (1, 2, 3):
        c = pltpu.make_async_remote_copy(
            src_ref=part,
            dst_ref=land_m.at[off - 1],
            send_sem=send_m.at[off - 1],
            recv_sem=recv_m.at[off - 1],
            **peer(cube * 4 + (spot + off) % 4),
        )
        c.start()
        mates.append(c)

    for c in second:
        c.wait()
    planar[0] = base[:, 0, :].astype(jnp.float32)
    planar[1] = base[:, 1, :].astype(jnp.float32)

    for i, c in enumerate(mates):
        c.wait_recv()
        cube_sum += land_m[i].astype(jnp.float32)

    def sum_arrived(i):
        pltpu.make_async_copy(land_s.at[i], land_s.at[i], recv_s.at[i]).wait()

    def gate_copies(gate):
        copies = []
        for cube_to, place in GATES[gate]:
            near_last = cube_to * 4 > gate
            for k in (3, 2, 1, 0) if near_last else (0, 1, 2, 3):
                copies.append(
                    pltpu.make_async_remote_copy(
                        src_ref=gate_sum,
                        dst_ref=land_s.at[place],
                        send_sem=send_s.at[len(copies)],
                        recv_sem=recv_s.at[place],
                        **peer(cube_to * 4 + k),
                    )
                )
        return copies

    for gate in GATES:
        @pl.when(me == gate)
        def _():
            outgoing = cube_sum
            if gate == RELAY:
                sum_arrived(0)
                outgoing += land_s[0].astype(jnp.float32)
            gate_sum[...] = outgoing.astype(jnp.bfloat16)
            for c in gate_copies(gate):
                c.start()

    for c in third:
        c.wait()

    @pl.when(me != RELAY)
    def _():
        sum_arrived(0)

    @pl.when(cube < 2)
    def _():
        sum_arrived(2)

    sum_arrived(1)
    shrunk = cube_sum
    for i in range(3):
        shrunk += land_s[i].astype(jnp.float32)
    swapped = pltpu.roll(shrunk, 64, 1)
    lhs = [
        jnp.where(keep, jnp.where(lane_low, shrunk, swapped), 0.0).astype(jnp.bfloat16),
        jnp.where(keep, jnp.where(lane_low, swapped, shrunk), 0.0).astype(jnp.bfloat16),
    ]
    narrowed = jnp.zeros((64, 128), jnp.float32)
    for k in range(13):
        cols = pl.ds(k * 256, 256)
        gate = dot(lhs[0], jnp.concatenate([expand_up[0, 0, :, cols], expand_up[1, 0, :, cols]], axis=0))
        up = dot(lhs[1], jnp.concatenate([expand_up[0, 1, :, cols], expand_up[1, 1, :, cols]], axis=0))
        gate += planar[0, :, cols]
        up += planar[1, :, cols]
        h = (gate / (1.0 + jnp.exp(-gate)) * up).astype(jnp.bfloat16)
        hidden[:, cols] = h
        narrowed += nt_dot(h, shrink_down[:, cols])

    turned = pltpu.roll(narrowed, 64, 1)
    low = jnp.where(second_slot, turned, narrowed)[:32]
    high = jnp.where(second_slot, narrowed, turned)[32:]
    part_down[...] = jnp.where(lane_low[:32], low, high).astype(jnp.bfloat16)
    copies_c = []
    for i in range(n - 1):
        c = pltpu.make_async_remote_copy(
            src_ref=part_down,
            dst_ref=land_c.at[me],
            send_sem=send_c.at[i],
            recv_sem=recv_c,
            **peer(i + jnp.where(me <= i, 1, 0)),
        )
        c.start()
        copies_c.append(c)
    land_c[me] = part_down[...]

    for c in mates:
        c.wait_send()
    for gate in GATES:
        @pl.when(me == gate)
        def _():
            for c in gate_copies(gate):
                c.wait_send()

    fifteen = land_c.at[pl.ds(0, n - 1)]
    pltpu.make_async_copy(fifteen, fifteen, recv_c).wait()
    packed = land_c[0].astype(jnp.float32)
    for i in range(1, n):
        packed += land_c[i].astype(jnp.float32)
    other = pltpu.roll(packed, 64, 1)
    spread = jnp.concatenate(
        [jnp.where(lane_low[:32], packed, other), jnp.where(lane_low[:32], other, packed)], axis=0
    )
    reduced[...] = jnp.where(keep, spread, 0.0).astype(jnp.bfloat16)
    for c in copies_c:
        c.wait_send()


def finish(hidden_in, reduced, expand_down, hidden_out, down_out, down, sem):
    rows = 16
    moves = []
    for i in range(4):
        part = pl.ds(i * rows, rows)
        c = pltpu.make_async_copy(hidden_in.at[part], hidden_out.at[part], sem.at[i])
        c.start()
        moves.append(c)
    down[...] = dot(reduced[...], expand_down[...]).astype(jnp.bfloat16)
    c = pltpu.make_async_copy(down, down_out, sem.at[4])
    c.start()
    for m in moves:
        m.wait()
    c.wait()


def per_device(
    tokens, gate_up_base, shrink_gate_up, expand_gate_up, shrink_down, expand_down, token_slot
):
    shrink_up = jnp.swapaxes(shrink_gate_up, 2, 3).reshape(256, 1024)
    down_t = jnp.swapaxes(shrink_down, 1, 2).reshape(128, 3328)
    expand_d = expand_down.reshape(128, 1024)
    slot = token_slot.reshape(1, 64)
    operands = [
        pltpu.with_memory_space_constraint(x, pltpu.HBM)
        for x in (tokens, gate_up_base, shrink_up, expand_gate_up, down_t, slot)
    ]
    bf, f32 = jnp.bfloat16, jnp.float32
    dma = pltpu.SemaphoreType.DMA
    hidden, reduced = pl.pallas_call(
        kernel,
        out_shape=(
            jax.ShapeDtypeStruct((64, 3328), bf),
            jax.ShapeDtypeStruct((64, 128), bf),
        ),
        in_specs=[pl.BlockSpec(memory_space=pltpu.HBM)] * 6,
        out_specs=[pl.BlockSpec(memory_space=pltpu.VMEM)] * 2,
        scratch_shapes=[
            pltpu.VMEM((64, 1024), bf),
            pltpu.VMEM((64, 2, 3328), bf),
            pltpu.VMEM((256, 1024), bf),
            pltpu.VMEM((2, 2, 64, 3328), bf),
            pltpu.VMEM((128, 3328), bf),
            pltpu.VMEM((1, 64), jnp.int32),
            pltpu.VMEM((2, 64, 3328), f32),
            pltpu.VMEM((64, 128), bf),
            pltpu.VMEM((3, 64, 128), bf),
            pltpu.VMEM((64, 128), bf),
            pltpu.VMEM((3, 64, 128), bf),
            pltpu.VMEM((32, 128), bf),
            pltpu.VMEM((16, 32, 128), bf),
            dma((6,)),
            dma((3,)),
            dma((3,)),
            dma((8,)),
            dma((3,)),
            dma((15,)),
            dma,
        ],
        compiler_params=pltpu.CompilerParams(
            collective_id=0, has_side_effects=True, vmem_limit_bytes=12 * 2**20
        ),
    )(*operands)
    return pl.pallas_call(
        finish,
        out_shape=(
            jax.ShapeDtypeStruct((64, 3328), bf),
            jax.ShapeDtypeStruct((64, 1024), bf),
        ),
        in_specs=[
            pl.BlockSpec(memory_space=pl.ANY),
            pl.BlockSpec(memory_space=pltpu.VMEM),
            pl.BlockSpec(memory_space=pltpu.VMEM),
        ],
        out_specs=[pl.BlockSpec(memory_space=pl.ANY)] * 2,
        scratch_shapes=[pltpu.VMEM((64, 1024), bf), dma((5,))],
        compiler_params=pltpu.CompilerParams(vmem_limit_bytes=4 * 2**20),
    )(hidden, reduced, expand_d)


def solution(mesh):
    placed = (
        P("dp", "tensor"),
        P("dp", None, "tensor"),
        P("dp", None, "tensor", None),
        P("dp", None, None, "tensor"),
        P("dp", "tensor", None),
        P("dp", None, "tensor"),
        P("dp"),
    )
    return jax.shard_map(
        per_device,
        mesh=mesh,
        in_specs=placed,
        out_specs=(P("dp", "tensor"), P("dp", "tensor")),
        check_vma=False,
    )
```

time: 39.5 us -> 32.1 us (0.81)
  the two profiles are of different devices: /device:TPU:6 before, /device:TPU:32 now
where the time goes in v2:
time: 32.1 us; the launch traced here: 32 us
  Pallas kernels  31.3 us (98%)
  between operations  0.66 us (2%)
    pallas_call x1, Pallas kernels, per_device(): pl.pallas_call(kernel, out_shape=(jax.ShapeDtypeStruct((64, 3328), bf), j...  30.4 us
    pallas_call x1, Pallas kernels, per_device(): pl.pallas_call(finish, out_shape=(jax.ShapeDtypeStruct((64, 3328), bf), j...  0.88 us

profile of v2, /device:TPU:32, one launch (start us, length us, event | category | flops | bytes accessed | tf_op | source)
XLA Modules:
  0.0 32.0 jit_solution(6978466043430855727)
XLA Ops:
  0.6 0.0 copy-start
  0.6 30.4 %shard_map.86 = (bf16[64,3328]{1,0:T(8,128)(2,1)S(1)}, bf16[64,128]{1,0:T(8,128)(2,1)S(1)}) custom-call(bf16[64,1024]{1,0:T(8,128)(2,1)} %tokens_hbm.1, bf16[64,2,3328]{2,1,0:T(2,128)(2,1)} %base_hbm.1, bf16[256,1024]{1,0:T(8,128)(2,1)} %bitcast.10, bf16[2,2,64,3328]{3,2,1,0:T(8,128)(2,1)} %expand_up_hbm.1, bf16[128,3328]{1,0:T(8,128)(2,1)} %bitcast.9, ...), custom_call_target="tpu_custom_call" | custom-call | tf_op jit(solution)/shard_map/pallas_call | solution.py:244
  31.1 0.0 copy-done
  31.1 0.9 %shard_map.87 = (bf16[64,3328]{1,0:T(8,128)(2,1)}, bf16[64,1024]{1,0:T(8,128)(2,1)}) custom-call(bf16[64,3328]{1,0:T(8,128)(2,1)S(1)} %get-tuple-element.4.hidden_in, bf16[64,128]{1,0:T(8,128)(2,1)S(1)} %get-tuple-element.5.reduced, bf16[128,1024]{1,0:T(8,128)(2,1)S(1)} %bitcast.8), custom_call_target="tpu_custom_call" | custom-call | tf_op jit(solution)/shard_map/pallas_call | solution.py:278
Async XLA Ops:
  0.6 30.5 %copy-start = (bf16[2,64,1024]{2,1,0:T(8,128)(2,1)S(1)}, bf16[2,64,1024]{2,1,0:T(8,128)(2,1)}, u32[]{:S(2)}) copy-start(bf16[2,64,1024]{2,1,0:T(8,128)(2,1)} %param.12) | copy-start | bytes 786436

commit v3 on v2

--- a/solution.py
+++ b/solution.py
@@ -19,16 +19,16 @@
     return jnp.dot(a, b, preferred_element_type=jnp.float32)
 
 
+CUBE = [tuple(range(4 * c, 4 * c + 4)) for c in range(4)]
+RELAY, FEED = 4, 3
 GATES = {
-    3: ((1, 0),),
-    4: ((0, 2),),
-    7: ((2, 0), (3, 1)),
-    8: ((1, 1), (0, 1)),
-    11: ((3, 0),),
-    12: ((2, 1), (1, 2)),
-    15: ((0, 0),),
+    FEED: [(RELAY, 0)],
+    RELAY: [(11, 0), (12, 1), (10, 0), (13, 1), (9, 0), (14, 1), (8, 0), (15, 1)] + [(z, 2) for z in (3, 2, 1, 0)],
+    8: [(z, 1) for z in CUBE[1] + CUBE[0]],
+    11: [(z, 0) for z in CUBE[3][::-1]],
+    12: [(z, 2) for z in CUBE[1]] + [(z, 1) for z in CUBE[2]],
+    15: [(z, 0) for z in CUBE[0]],
 }
-RELAY = 7
 
 
 def kernel(
@@ -56,22 +56,35 @@
         pl.semaphore_signal(barrier, inc=1, **peer(z))
 
     barrier = pltpu.get_barrier_semaphore()
-    for dst in range(4):
-        @pl.when(cube == dst)
-        def _():
-            for gate, targets in GATES.items():
-                if dst in [c for c, _ in targets]:
-                    greet(gate)
+    @pl.when(cube >= 2)
+    def _():
+        greet(RELAY)
+        greet(jnp.where(cube == 2, 12, 11))
+
     for off in (1, 2, 3):
         greet(cube * 4 + (spot + off) % 4)
+
+    @pl.when(cube < 2)
+    def _():
+        greet(8)
+        greet(jnp.where(cube == 0, 15, 12))
+
+        @pl.when(cube == 0)
+        def _():
+            greet(RELAY)
+
+        @pl.when(me == RELAY)
+        def _():
+            greet(FEED)
 
     first = [load(0, tokens_hbm, tokens), load(1, shrink_up_hbm, shrink_up), load(2, slot_hbm, slot)]
     second = [load(3, base_hbm, base), load(4, expand_up_hbm, expand_up)]
     third = [load(5, shrink_down_hbm, shrink_down)]
 
-    @pl.when(cube >= 2)
-    def _():
-        land_s[2] = jnp.zeros((64, 128), jnp.bfloat16)
+    for i, bare in ((0, (cube == RELAY // 4) & (me != RELAY)), (2, cube >= 2)):
+        @pl.when(bare)
+        def _():
+            land_s[i] = jnp.zeros((64, 128), jnp.bfloat16)
 
     for c in first:
         c.wait()
@@ -84,24 +97,28 @@
 
     both = nt_dot(tokens[...], shrink_up[...])
     cube_sum = jnp.where(second_slot, both[:, 128:], both[:, :128])
+    own_part = cube_sum
     part[...] = cube_sum.astype(jnp.bfloat16)
 
-    greetings = 3
-    for gate, targets in GATES.items():
-        greetings += jnp.where(me == gate, 4 * len(targets), 0)
-    pl.semaphore_wait(barrier, greetings)
-
-    mates = []
-    for off in (1, 2, 3):
-        c = pltpu.make_async_remote_copy(
+    mates = [
+        pltpu.make_async_remote_copy(
             src_ref=part,
             dst_ref=land_m.at[off - 1],
             send_sem=send_m.at[off - 1],
             recv_sem=recv_m.at[off - 1],
             **peer(cube * 4 + (spot + off) % 4),
         )
-        c.start()
-        mates.append(c)
+        for off in (1, 2, 3)
+    ]
+
+    @pl.when(me != RELAY)
+    def _():
+        greetings = 3
+        for gate, targets in GATES.items():
+            greetings += jnp.where(me == gate, len(targets), 0)
+        pl.semaphore_wait(barrier, greetings)
+        for c in mates:
+            c.start()
 
     for c in second:
         c.wait()
@@ -116,36 +133,38 @@
         pltpu.make_async_copy(land_s.at[i], land_s.at[i], recv_s.at[i]).wait()
 
     def gate_copies(gate):
-        copies = []
-        for cube_to, place in GATES[gate]:
-            near_last = cube_to * 4 > gate
-            for k in (3, 2, 1, 0) if near_last else (0, 1, 2, 3):
-                copies.append(
-                    pltpu.make_async_remote_copy(
-                        src_ref=gate_sum,
-                        dst_ref=land_s.at[place],
-                        send_sem=send_s.at[len(copies)],
-                        recv_sem=recv_s.at[place],
-                        **peer(cube_to * 4 + k),
-                    )
-                )
-        return copies
+        return [
+            pltpu.make_async_remote_copy(
+                src_ref=gate_sum.at[1 if z < gate and gate == RELAY else 0],
+                dst_ref=land_s.at[place],
+                send_sem=send_s.at[i],
+                recv_sem=recv_s.at[place],
+                **peer(z),
+            )
+            for i, (z, place) in enumerate(GATES[gate])
+        ]
 
     for gate in GATES:
         @pl.when(me == gate)
         def _():
-            outgoing = cube_sum
+            gate_sum[0] = cube_sum.astype(jnp.bfloat16)
             if gate == RELAY:
+                gate_sum[1] = cube_sum.astype(jnp.bfloat16)
                 sum_arrived(0)
-                outgoing += land_s[0].astype(jnp.float32)
-            gate_sum[...] = outgoing.astype(jnp.bfloat16)
+                fed = land_s[0].astype(jnp.float32)
+                gate_sum[0] = (cube_sum + fed).astype(jnp.bfloat16)
+                part[...] = (own_part + fed).astype(jnp.bfloat16)
+                pl.semaphore_wait(barrier, 3 + len(GATES[gate]))
             for c in gate_copies(gate):
                 c.start()
+            if gate == RELAY:
+                for c in mates:
+                    c.start()
 
     for c in third:
         c.wait()
 
-    @pl.when(me != RELAY)
+    @pl.when(cube != RELAY // 4)
     def _():
         sum_arrived(0)
 
@@ -162,7 +181,6 @@
         jnp.where(keep, jnp.where(lane_low, shrunk, swapped), 0.0).astype(jnp.bfloat16),
         jnp.where(keep, jnp.where(lane_low, swapped, shrunk), 0.0).astype(jnp.bfloat16),
     ]
-    narrowed = jnp.zeros((64, 128), jnp.float32)
     for k in range(13):
         cols = pl.ds(k * 256, 256)
         gate = dot(lhs[0], jnp.concatenate([expand_up[0, 0, :, cols], expand_up[1, 0, :, cols]], axis=0))
@@ -171,7 +189,7 @@
         up += planar[1, :, cols]
         h = (gate / (1.0 + jnp.exp(-gate)) * up).astype(jnp.bfloat16)
         hidden[:, cols] = h
-        narrowed += nt_dot(h, shrink_down[:, cols])
+    narrowed = nt_dot(hidden[...], shrink_down[...])
 
     turned = pltpu.roll(narrowed, 64, 1)
     low = jnp.where(second_slot, turned, narrowed)[:32]
@@ -259,14 +277,14 @@
             pltpu.VMEM((2, 64, 3328), f32),
             pltpu.VMEM((64, 128), bf),
             pltpu.VMEM((3, 64, 128), bf),
-            pltpu.VMEM((64, 128), bf),
+            pltpu.VMEM((2, 64, 128), bf),
             pltpu.VMEM((3, 64, 128), bf),
             pltpu.VMEM((32, 128), bf),
             pltpu.VMEM((16, 32, 128), bf),
             dma((6,)),
             dma((3,)),
             dma((3,)),
-            dma((8,)),
+            dma((12,)),
             dma((3,)),
             dma((15,)),
             dma,

time: 32.1 us -> 30.4 us (0.947)
  the two profiles are of different devices: /device:TPU:32 before, /device:TPU:6 now
where the time goes in v3:
time: 30.4 us; the launch traced here: 30.2 us
  Pallas kernels  29.6 us (97%)
  between operations  0.66 us (2%)
    pallas_call x1, Pallas kernels, per_device(): pl.pallas_call(kernel, out_shape=(jax.ShapeDtypeStruct((64, 3328), bf), j...  28.7 us
    pallas_call x1, Pallas kernels, per_device(): pl.pallas_call(finish, out_shape=(jax.ShapeDtypeStruct((64, 3328), bf), j...  0.88 us

profile of v3, /device:TPU:6, one launch (start us, length us, event | category | flops | bytes accessed | tf_op | source)
XLA Modules:
  0.0 30.2 jit_solution(12178642001312260100)
XLA Ops:
  0.6 0.0 copy-start
  0.6 28.7 %shard_map.86 = (bf16[64,3328]{1,0:T(8,128)(2,1)S(1)}, bf16[64,128]{1,0:T(8,128)(2,1)S(1)}) custom-call(bf16[64,1024]{1,0:T(8,128)(2,1)} %tokens_hbm.1, bf16[64,2,3328]{2,1,0:T(2,128)(2,1)} %base_hbm.1, bf16[256,1024]{1,0:T(8,128)(2,1)} %bitcast.10, bf16[2,2,64,3328]{3,2,1,0:T(8,128)(2,1)} %expand_up_hbm.1, bf16[128,3328]{1,0:T(8,128)(2,1)} %bitcast.9, ...), custom_call_target="tpu_custom_call" | custom-call | tf_op jit(solution)/shard_map/pallas_call | solution.py:262
  29.4 0.0 copy-done
  29.4 0.9 %shard_map.87 = (bf16[64,3328]{1,0:T(8,128)(2,1)}, bf16[64,1024]{1,0:T(8,128)(2,1)}) custom-call(bf16[64,3328]{1,0:T(8,128)(2,1)S(1)} %get-tuple-element.4.hidden_in, bf16[64,128]{1,0:T(8,128)(2,1)S(1)} %get-tuple-element.5.reduced, bf16[128,1024]{1,0:T(8,128)(2,1)S(1)} %bitcast.8), custom_call_target="tpu_custom_call" | custom-call | tf_op jit(solution)/shard_map/pallas_call | solution.py:296
Async XLA Ops:
  0.6 28.7 %copy-start = (bf16[2,64,1024]{2,1,0:T(8,128)(2,1)S(1)}, bf16[2,64,1024]{2,1,0:T(8,128)(2,1)}, u32[]{:S(2)}) copy-start(bf16[2,64,1024]{2,1,0:T(8,128)(2,1)} %param.12) | copy-start | bytes 786436

commit v4 on v3

--- a/solution.py
+++ b/solution.py
@@ -35,7 +35,7 @@
     tokens_hbm, base_hbm, shrink_up_hbm, expand_up_hbm, shrink_down_hbm, slot_hbm,
     hidden, reduced,
     tokens, base, shrink_up, expand_up, shrink_down, slot,
-    planar,
+    planar, shrink_down_t,
     part, land_m, gate_sum, land_s, part_down, land_c,
     in_sem, send_m, recv_m, send_s, recv_s, send_c, recv_c,
 ):
@@ -163,6 +163,7 @@
 
     for c in third:
         c.wait()
+    shrink_down_t[...] = shrink_down[...].T
 
     @pl.when(cube != RELAY // 4)
     def _():
@@ -189,7 +190,7 @@
         up += planar[1, :, cols]
         h = (gate / (1.0 + jnp.exp(-gate)) * up).astype(jnp.bfloat16)
         hidden[:, cols] = h
-    narrowed = nt_dot(hidden[...], shrink_down[...])
+    narrowed = dot(hidden[...], shrink_down_t[...])
 
     turned = pltpu.roll(narrowed, 64, 1)
     low = jnp.where(second_slot, turned, narrowed)[:32]
@@ -275,6 +276,7 @@
             pltpu.VMEM((128, 3328), bf),
             pltpu.VMEM((1, 64), jnp.int32),
             pltpu.VMEM((2, 64, 3328), f32),
+            pltpu.VMEM((3328, 128), bf),
             pltpu.VMEM((64, 128), bf),
             pltpu.VMEM((3, 64, 128), bf),
             pltpu.VMEM((2, 64, 128), bf),

time: 30.4 us -> 30.3 us (level)
  no operation moved by 1% of the time
where the time goes in v4:
time: 30.3 us; the launch traced here: 30.1 us
  Pallas kernels  29.4 us (97%)
  between operations  0.66 us (2%)
    pallas_call x1, Pallas kernels, per_device(): pl.pallas_call(kernel, out_shape=(jax.ShapeDtypeStruct((64, 3328), bf), j...  28.5 us
    pallas_call x1, Pallas kernels, per_device(): pl.pallas_call(finish, out_shape=(jax.ShapeDtypeStruct((64, 3328), bf), j...  0.88 us

profile of v4, /device:TPU:6, one launch (start us, length us, event | category | flops | bytes accessed | tf_op | source)
XLA Modules:
  0.0 30.1 jit_solution(3308086108666561029)
XLA Ops:
  0.6 0.0 copy-start
  0.6 28.5 %shard_map.86 = (bf16[64,3328]{1,0:T(8,128)(2,1)S(1)}, bf16[64,128]{1,0:T(8,128)(2,1)S(1)}) custom-call(bf16[64,1024]{1,0:T(8,128)(2,1)} %tokens_hbm.1, bf16[64,2,3328]{2,1,0:T(2,128)(2,1)} %base_hbm.1, bf16[256,1024]{1,0:T(8,128)(2,1)} %bitcast.10, bf16[2,2,64,3328]{3,2,1,0:T(8,128)(2,1)} %expand_up_hbm.1, bf16[128,3328]{1,0:T(8,128)(2,1)} %bitcast.9, ...), custom_call_target="tpu_custom_call" | custom-call | tf_op jit(solution)/shard_map/pallas_call | solution.py:263
  29.2 0.0 copy-done
  29.2 0.9 %shard_map.87 = (bf16[64,3328]{1,0:T(8,128)(2,1)}, bf16[64,1024]{1,0:T(8,128)(2,1)}) custom-call(bf16[64,3328]{1,0:T(8,128)(2,1)S(1)} %get-tuple-element.4.hidden_in, bf16[64,128]{1,0:T(8,128)(2,1)S(1)} %get-tuple-element.5.reduced, bf16[128,1024]{1,0:T(8,128)(2,1)S(1)} %bitcast.8), custom_call_target="tpu_custom_call" | custom-call | tf_op jit(solution)/shard_map/pallas_call | solution.py:298
Async XLA Ops:
  0.6 28.6 %copy-start = (bf16[2,64,1024]{2,1,0:T(8,128)(2,1)S(1)}, bf16[2,64,1024]{2,1,0:T(8,128)(2,1)}, u32[]{:S(2)}) copy-start(bf16[2,64,1024]{2,1,0:T(8,128)(2,1)} %param.12) | copy-start | bytes 786436

commit v5 on v4

--- a/solution.py
+++ b/solution.py
@@ -100,16 +100,21 @@
     own_part = cube_sum
     part[...] = cube_sum.astype(jnp.bfloat16)
 
-    mates = [
-        pltpu.make_async_remote_copy(
-            src_ref=part,
-            dst_ref=land_m.at[off - 1],
-            send_sem=send_m.at[off - 1],
-            recv_sem=recv_m.at[off - 1],
-            **peer(cube * 4 + (spot + off) % 4),
+    mates = []
+    for k in range(3):
+        up = k + jnp.where(spot <= k, 1, 0)
+        down = 3 - k - jnp.where(3 - spot <= k, 1, 0)
+        to = jnp.where(cube == 0, down, up)
+        place = (to - spot + 4) % 4 - 1
+        mates.append(
+            pltpu.make_async_remote_copy(
+                src_ref=part,
+                dst_ref=land_m.at[place],
+                send_sem=send_m.at[k],
+                recv_sem=recv_m.at[place],
+                **peer(cube * 4 + to),
+            )
         )
-        for off in (1, 2, 3)
-    ]
 
     @pl.when(me != RELAY)
     def _():
@@ -125,8 +130,8 @@
     planar[0] = base[:, 0, :].astype(jnp.float32)
     planar[1] = base[:, 1, :].astype(jnp.float32)
 
-    for i, c in enumerate(mates):
-        c.wait_recv()
+    for i in range(3):
+        pltpu.make_async_copy(land_m.at[i], land_m.at[i], recv_m.at[i]).wait()
         cube_sum += land_m[i].astype(jnp.float32)
 
     def sum_arrived(i):

time: 30.3 us -> 30.2 us (level)
  no operation moved by 1% of the time
where the time goes in v5:
time: 30.2 us; the launch traced here: 30.1 us
  Pallas kernels  29.4 us (97%)
  between operations  0.66 us (2%)
    pallas_call x1, Pallas kernels, per_device(): pl.pallas_call(kernel, out_shape=(jax.ShapeDtypeStruct((64, 3328), bf), j...  28.5 us
    pallas_call x1, Pallas kernels, per_device(): pl.pallas_call(finish, out_shape=(jax.ShapeDtypeStruct((64, 3328), bf), j...  0.88 us

profile of v5, /device:TPU:6, one launch (start us, length us, event | category | flops | bytes accessed | tf_op | source)
XLA Modules:
  0.0 30.1 jit_solution(16968224096553240512)
XLA Ops:
  0.6 0.0 copy-start
  0.6 28.5 %shard_map.86 = (bf16[64,3328]{1,0:T(8,128)(2,1)S(1)}, bf16[64,128]{1,0:T(8,128)(2,1)S(1)}) custom-call(bf16[64,1024]{1,0:T(8,128)(2,1)} %tokens_hbm.1, bf16[64,2,3328]{2,1,0:T(2,128)(2,1)} %base_hbm.1, bf16[256,1024]{1,0:T(8,128)(2,1)} %bitcast.10, bf16[2,2,64,3328]{3,2,1,0:T(8,128)(2,1)} %expand_up_hbm.1, bf16[128,3328]{1,0:T(8,128)(2,1)} %bitcast.9, ...), custom_call_target="tpu_custom_call" | custom-call | tf_op jit(solution)/shard_map/pallas_call | solution.py:268
  29.2 0.0 copy-done
  29.2 0.9 %shard_map.87 = (bf16[64,3328]{1,0:T(8,128)(2,1)}, bf16[64,1024]{1,0:T(8,128)(2,1)}) custom-call(bf16[64,3328]{1,0:T(8,128)(2,1)S(1)} %get-tuple-element.4.hidden_in, bf16[64,128]{1,0:T(8,128)(2,1)S(1)} %get-tuple-element.5.reduced, bf16[128,1024]{1,0:T(8,128)(2,1)S(1)} %bitcast.8), custom_call_target="tpu_custom_call" | custom-call | tf_op jit(solution)/shard_map/pallas_call | solution.py:303
Async XLA Ops:
  0.6 28.6 %copy-start = (bf16[2,64,1024]{2,1,0:T(8,128)(2,1)S(1)}, bf16[2,64,1024]{2,1,0:T(8,128)(2,1)}, u32[]{:S(2)}) copy-start(bf16[2,64,1024]{2,1,0:T(8,128)(2,1)} %param.12) | copy-start | bytes 786436

commit v6 on v5

--- a/solution.py
+++ b/solution.py
@@ -61,6 +61,8 @@
         greet(RELAY)
         greet(jnp.where(cube == 2, 12, 11))
 
+    first = [load(0, tokens_hbm, tokens), load(1, shrink_up_hbm, shrink_up), load(2, slot_hbm, slot)]
+
     for off in (1, 2, 3):
         greet(cube * 4 + (spot + off) % 4)
 
@@ -77,7 +79,6 @@
         def _():
             greet(FEED)
 
-    first = [load(0, tokens_hbm, tokens), load(1, shrink_up_hbm, shrink_up), load(2, slot_hbm, slot)]
     second = [load(3, base_hbm, base), load(4, expand_up_hbm, expand_up)]
     third = [load(5, shrink_down_hbm, shrink_down)]
 

time: 30.2 us -> 30.2 us (level)
  no operation moved by 1% of the time
where the time goes in v6:
time: 30.2 us; the launch traced here: 30.1 us
  Pallas kernels  29.4 us (97%)
  between operations  0.66 us (2%)
    pallas_call x1, Pallas kernels, per_device(): pl.pallas_call(kernel, out_shape=(jax.ShapeDtypeStruct((64, 3328), bf), j...  28.6 us
    pallas_call x1, Pallas kernels, per_device(): pl.pallas_call(finish, out_shape=(jax.ShapeDtypeStruct((64, 3328), bf), j...  0.88 us

profile of v6, /device:TPU:6, one launch (start us, length us, event | category | flops | bytes accessed | tf_op | source)
XLA Modules:
  0.0 30.1 jit_solution(4790750071512991599)
XLA Ops:
  0.6 0.0 copy-start
  0.6 28.6 %shard_map.86 = (bf16[64,3328]{1,0:T(8,128)(2,1)S(1)}, bf16[64,128]{1,0:T(8,128)(2,1)S(1)}) custom-call(bf16[64,1024]{1,0:T(8,128)(2,1)} %tokens_hbm.1, bf16[64,2,3328]{2,1,0:T(2,128)(2,1)} %base_hbm.1, bf16[256,1024]{1,0:T(8,128)(2,1)} %bitcast.10, bf16[2,2,64,3328]{3,2,1,0:T(8,128)(2,1)} %expand_up_hbm.1, bf16[128,3328]{1,0:T(8,128)(2,1)} %bitcast.9, ...), custom_call_target="tpu_custom_call" | custom-call | tf_op jit(solution)/shard_map/pallas_call | solution.py:269
  29.2 0.0 copy-done
  29.2 0.9 %shard_map.87 = (bf16[64,3328]{1,0:T(8,128)(2,1)}, bf16[64,1024]{1,0:T(8,128)(2,1)}) custom-call(bf16[64,3328]{1,0:T(8,128)(2,1)S(1)} %get-tuple-element.4.hidden_in, bf16[64,128]{1,0:T(8,128)(2,1)S(1)} %get-tuple-element.5.reduced, bf16[128,1024]{1,0:T(8,128)(2,1)S(1)} %bitcast.8), custom_call_target="tpu_custom_call" | custom-call | tf_op jit(solution)/shard_map/pallas_call | solution.py:304
Async XLA Ops:
  0.6 28.6 %copy-start = (bf16[2,64,1024]{2,1,0:T(8,128)(2,1)S(1)}, bf16[2,64,1024]{2,1,0:T(8,128)(2,1)}, u32[]{:S(2)}) copy-start(bf16[2,64,1024]{2,1,0:T(8,128)(2,1)} %param.12) | copy-start | bytes 786436
